TPU v7x, 32 devices: a whole 2x2x4 slice. The times are simulated.
32 devices in a mesh: seq: 8 (over z, x), exp: 4 (over y, core).
Axes of the slice: x: 2, y: 2, z: 4, core: 2. Of those that a mesh axis runs over, the one named last changes fastest.
Arguments:
- x_in: bfloat16 [512, 8192], P('seq', 'exp'), may hold values from -6 to 6
- z_in: bfloat16 [512, 8192], P('seq', 'exp'), may hold values from -6 to 6
- conv_weight: float32 [4, 8192], P(None, 'exp'), may hold values from -3 to 3
- conv_bias: float32 [8192], P('exp'), may hold values from -3 to 3
- x_proj: bfloat16 [8192, 544], P('exp'), may hold values from -0.0625 to 0.0625
- dt_proj: bfloat16 [512, 8192], P(None, 'exp'), may hold values from -0.25 to 0.25
- dt_bias: float32 [8192], P('exp'), may hold values from -7 to -2.3
- a_log: float32 [8192, 16], P('exp'), may hold values from -6 to 0
- d_skip: float32 [8192], P('exp'), may hold values from 0.5 to 1.5
- out_proj: bfloat16 [8192, 4096], P('exp', 'seq'), may hold values from -0.0625 to 0.0625
- resid: bfloat16 [512, 4096], P('seq', 'exp'), may hold values from -8 to 8
- norm_gain: float32 [4096], replicated, may hold values from 0.5 to 1.5
- routes: int32 [512, 2], P('seq'), may hold values from 0 to 3, all different within a row; in each aligned block of 64 rows (0 to 63, 64 to 127, ...) at most 34 rows name the same one
- route_gate: float32 [512, 2], P('seq'), may hold values from 0.1 to 0.9
- w_gate: bfloat16 [4, 4096, 12288], P('exp', None, 'seq'), may hold values from -0.09375 to 0.09375
- w_up: bfloat16 [4, 4096, 12288], P('exp', None, 'seq'), may hold values from -0.09375 to 0.09375
- w_down: bfloat16 [4, 12288, 4096], P('exp', 'seq'), may hold values from -0.078125 to 0.078125
Outputs:
- layer_out: bfloat16 [512, 4096], P('seq', 'exp')
Inputs may be any that keep to these rules, and one draw needn't show every extreme that they name: `routes`: the 2 experts of a position differ; among the 64 positions of one index of seq no expert is named more than 34 times, and in some such block one expert is named exactly 34 times.
All inputs are finite; a program needn't handle non-finite values.
Results may differ from a plain program's by a relative error of at most 0.008.
Values may be sent and summed in bfloat16 or wider, within the bound.
No kernel may reach another device: no remote copies, remote signals or barrier semaphores. Data moves between devices by JAX's collectives and lax.ppermute only.
A program may use at most 128 MiB of HBM per device.

v0:
```python
import math

import jax
import jax.numpy as jnp
from jax import lax
from jax.sharding import PartitionSpec as P

eps = 1e-05


def passed_along(block, axis, distance):
    devices = range(lax.axis_size(axis))
    route = [(i - distance, i) for i in devices if i - distance in devices]
    return lax.ppermute(block, axis, route)


def combine_pairs(earlier, later):
    return (earlier[0] * later[0], later[0] * earlier[1] + later[1])


def local_scan(step_size, drive_input, b_mat, c_mat, rates):
    row_count, channels = step_size.shape
    block = math.gcd(row_count, 16)
    block_count = row_count // block

    def advance(state, pieces):
        size_block, drive_block, b_block, c_block = pieces
        decay = jnp.exp(size_block[:, :, None] * rates[None])
        drive = drive_block[:, :, None] * b_block[:, None, :]
        products, sums = lax.associative_scan(combine_pairs, (decay, drive), axis=0)
        states = sums + products * state[None]
        outputs = jnp.sum(states * c_block[:, None, :], axis=2)
        return (states[-1], outputs)

    initial = jnp.zeros((channels, rates.shape[1]), jnp.float32)
    pieces = (
        step_size.reshape(block_count, block, channels),
        drive_input.reshape(block_count, block, channels),
        b_mat.reshape(block_count, block, -1),
        c_mat.reshape(block_count, block, -1),
    )
    final_state, outputs = lax.scan(advance, initial, pieces)
    return (final_state, outputs.reshape(row_count, channels))


def expert_hidden(rows_in, gate_w, up_w):
    gate = jnp.dot(rows_in, gate_w, preferred_element_type=jnp.float32)
    upper = jnp.dot(rows_in, up_w, preferred_element_type=jnp.float32)
    return (jax.nn.silu(gate) * upper).astype(jnp.bfloat16)


def per_device(
    x_in,
    z_in,
    conv_weight,
    conv_bias,
    x_proj,
    dt_proj,
    dt_bias,
    a_log,
    d_skip,
    out_proj,
    resid,
    norm_gain,
    routes,
    route_gate,
    w_gate,
    w_up,
    w_down,
):
    row_count, channels = x_in.shape
    tap_count = conv_weight.shape[0]
    earlier_rows = passed_along(x_in[row_count - tap_count + 1 :], "seq", 1)
    extended = jnp.concatenate([earlier_rows, x_in], axis=0).astype(jnp.float32)
    conv = jnp.zeros((row_count, channels), jnp.float32) + conv_bias[None, :]
    for tap in range(tap_count):
        conv = conv + conv_weight[tap][None, :] * extended[tap : tap + row_count]
    xconv = jax.nn.silu(conv).astype(jnp.bfloat16)
    partial_proj = jnp.dot(xconv, x_proj, preferred_element_type=jnp.float32)
    projected = lax.psum(partial_proj, "exp")
    low_rank = dt_proj.shape[0]
    state_count = a_log.shape[1]
    dt_low = projected[:, :low_rank].astype(jnp.bfloat16)
    b_mat = projected[:, low_rank : low_rank + state_count]
    c_mat = projected[:, low_rank + state_count :]
    step_size = jax.nn.softplus(
        jnp.dot(dt_low, dt_proj, preferred_element_type=jnp.float32) + dt_bias[None, :]
    )
    rates = -jnp.exp(a_log)
    xconv_f = xconv.astype(jnp.float32)
    end_state, local_out = local_scan(step_size, step_size * xconv_f, b_mat, c_mat, rates)
    size_total = jnp.sum(step_size, axis=0)
    all_totals, all_ends = (
        lax.all_gather(size_total[None], "seq", axis=0, tiled=True),
        lax.all_gather(end_state[None], "seq", axis=0, tiled=True),
    )
    position = lax.axis_index("seq")
    inclusive = jnp.cumsum(all_totals, axis=0)
    previous = lax.dynamic_index_in_dim(inclusive, jnp.maximum(position - 1, 0), 0, keepdims=False)
    previous = jnp.where(position > 0, previous, jnp.zeros_like(previous))
    tail = jnp.maximum(previous[None, :] - inclusive, 0.0)
    earlier_mask = (jnp.arange(all_totals.shape[0]) < position)[:, None, None]
    terms = jnp.exp(rates[None] * tail[:, :, None]) * all_ends
    incoming = jnp.sum(jnp.where(earlier_mask, terms, 0.0), axis=0)
    cumulative = jnp.cumsum(step_size, axis=0)
    carried = jnp.sum(
        c_mat[:, None, :] * jnp.exp(cumulative[:, :, None] * rates[None]) * incoming[None], axis=2
    )
    scanned = local_out + carried + d_skip[None, :] * xconv_f
    mixed = (scanned * jax.nn.silu(z_in.astype(jnp.float32))).astype(jnp.bfloat16)
    full_out = jnp.dot(
        mixed,
        lax.all_gather(out_proj, "seq", axis=1, tiled=True),
        preferred_element_type=jnp.float32,
    )
    mamba_out = lax.psum_scatter(full_out, "exp", scatter_dimension=1, tiled=True)
    hidden_state = (resid.astype(jnp.float32) + mamba_out).astype(jnp.bfloat16)
    feature_slice = hidden_state.shape[1]
    exp_count = lax.axis_size("exp")
    hidden_f = hidden_state.astype(jnp.float32)
    squares = lax.psum(jnp.sum(hidden_f * hidden_f, axis=1), "exp")
    scale = lax.rsqrt(squares / (feature_slice * exp_count) + eps)
    gain_slice = lax.dynamic_slice_in_dim(
        norm_gain, lax.axis_index("exp") * feature_slice, feature_slice, 0
    )
    outgoing_rows = (hidden_f * scale[:, None] * gain_slice[None, :]).astype(jnp.bfloat16)
    top_count = routes.shape[1]
    experts = w_gate.shape[0] * exp_count
    capacity = row_count * top_count * 17 // (16 * experts)
    flat_routes = routes.reshape(-1)
    onehot = (flat_routes[:, None] == jnp.arange(experts, dtype=jnp.int32)[None, :]).astype(
        jnp.int32
    )
    slots = jnp.sum((jnp.cumsum(onehot, axis=0) - 1) * onehot, axis=1)
    target = (flat_routes * capacity + slots).reshape(row_count, top_count)
    slot_ids = jnp.arange(experts * capacity, dtype=jnp.int32)
    dispatch = jnp.sum(
        (target[None, :, :] == slot_ids[:, None, None]).astype(jnp.int32), axis=2
    ).astype(jnp.bfloat16)
    outgoing = jnp.dot(dispatch, outgoing_rows, preferred_element_type=jnp.float32).astype(
        jnp.bfloat16
    )
    outgoing = outgoing.reshape(experts, capacity, feature_slice)
    arrived = lax.all_to_all(outgoing, "exp", split_axis=0, concat_axis=2, tiled=True)
    arrived = arrived.reshape(capacity, feature_slice * exp_count)
    activated = expert_hidden(
        lax.all_gather(arrived, "seq", axis=0, tiled=True), w_gate[0], w_up[0]
    )
    down_weight = w_down[0]
    returned = lax.psum_scatter(
        jnp.dot(activated, down_weight, preferred_element_type=jnp.float32).astype(jnp.bfloat16),
        "seq",
        scatter_dimension=0,
        tiled=True,
    )
    back = lax.all_to_all(returned[None], "exp", split_axis=2, concat_axis=0, tiled=True)
    flat_back = back.reshape(experts * capacity, feature_slice)
    choose = (target.T[:, :, None] == slot_ids[None, None, :]).astype(jnp.bfloat16)
    picked = jnp.dot(
        choose.reshape(top_count * row_count, experts * capacity),
        flat_back,
        preferred_element_type=jnp.float32,
    )
    picked = picked.reshape(top_count, row_count, feature_slice)
    moe = jnp.sum(route_gate.T[:, :, None] * picked, axis=0)
    return (hidden_state.astype(jnp.float32) + moe).astype(jnp.bfloat16)


def solution(mesh):
    return jax.shard_map(
        per_device,
        mesh=mesh,
        in_specs=(
            P("seq", "exp"),
            P("seq", "exp"),
            P(None, "exp"),
            P("exp"),
            P("exp", None),
            P(None, "exp"),
            P("exp"),
            P("exp", None),
            P("exp"),
            P("exp", "seq"),
            P("seq", "exp"),
            P(),
            P("seq", None),
            P("seq", None),
            P("exp", None, "seq"),
            P("exp", None, "seq"),
            P("exp", "seq", None),
        ),
        out_specs=P("seq", "exp"),
        check_vma=False,
    )
```

profile of v0, /device:TPU:5, one launch (start us, length us, event | category | flops | bytes accessed | tf_op | source)
XLA Modules:
  0.0 897.0 jit_solution(16311667731879861306)
XLA Ops:
  16.2 32.7 %all-reduce.20.cloned.1.call-done = f32[64,544]{1,0:T(8,128)} async-done(((f32[64,544]{1,0:T(8,128)}), f32[64,544]{1,0:T(8,128)}) %all-reduce.20.cloned.1.call-update) | async-done | bytes 139280 | tf_op jit(solution)/shard_map/psum | solution.py:80
  54.9 319.4 %while.12 = (s32[]{:T(128)}, f32[2048,16]{0,1:T(8,128)}, f32[4,16,2048]{2,1,0:T(8,128)}, f32[4,16,2048]{2,1,0:T(8,128)}, f32[4,16,16]{2,1,0:T(8,128)S(1)}, /*ind...) while((s32[]{:T(128)}, f32[2048,16]{0,1:T(8,128)}, ...), condition=%wide.region_3.4_spmd, body=%wide.region_1.3_spmd.sunk | while | flops 9273346 | bytes 108829648 | solution.py:42
  87.5 6.5 pad.158
  96.8 4.2 pad.154
  103.0 4.2 pad.153
  109.9 6.5 pad.156
  167.4 6.5 pad.158
  176.6 4.2 pad.154
  182.9 4.2 pad.153
  189.7 6.5 pad.156
  247.2 6.5 pad.158
  256.5 4.2 pad.154
  262.7 4.2 pad.153
  269.6 6.5 pad.156
  327.0 6.5 pad.158
  336.3 4.2 pad.154
  342.5 4.2 pad.153
  349.4 6.5 pad.156
  376.6 24.4 %all-gather = f32[16384]{0:T(1024)S(1)} all-gather(f32[2048]{0:T(1024)S(1)} %copy-done.26), channel_id=2, replica_groups=mesh['seq'=8,'exp'=4] {'seq'}, dimensions={0}, use_global_device_ids=true | all-gather | bytes 73728 | tf_op jit(solution)/shard_map/all_gather | solution.py:94
  401.2 14.3 %all-gather.9.cloned.1.call-done = f32[16384,16]{0,1:T(8,128)} async-done(((f32[2048,16]{0,1:T(8,128)}), f32[16384,16]{0,1:T(8,128)}) %all-gather.9.cloned.1.call-update) | async-done | bytes 1048592 | tf_op jit(solution)/shard_map/all_gather | solution.py:95
  421.4 223.5 %all-gather.7.cloned.1.call-done = bf16[2048,4096]{1,0:T(8,128)(2,1)} async-done(((bf16[2048,512]{1,0:T(8,128)(2,1)}), bf16[2048,4096]{1,0:T(8,128)(2,1)}) %all-gather.7.cloned.1.call-update) | async-done | bytes 16777232 | tf_op jit(solution)/shard_map/all_gather | solution.py:113
  644.9 9.8 %fusion.57 = f32[64,4096]{1,0:T(8,128)} fusion(bf16[64,2048]{1,0:T(8,128)(2,1)S(1)} %fusion.30, bf16[2048,4096]{1,0:T(8,128)(2,1)} %all-gather.7.cloned.1.call-done), kind=kOutput, calls=%fused_computation.114 | convolution fusion | flops 1073741824 | bytes 18087936 | tf_op jit(solution)/shard_map/dot_general | solution.py:111
  656.5 20.9 %reduce-scatter.4.cloned.1.call-done = f32[64,1024]{1,0:T(8,128)} async-done(((f32[64,4096]{1,0:T(8,128)}), f32[64,1024]{1,0:T(8,128)}) %reduce-scatter.4.cloned.1.call-update) | async-done | bytes 262160 | tf_op jit(solution)/shard_map/reduce_scatter | solution.py:116
  678.4 5.6 psum.15
  684.4 9.3 %all_to_all.30 = bf16[4,34,1024]{2,1,0:T(8,128)(2,1)S(1)} all-to-all(bf16[4,34,1024]{2,1,0:T(8,128)(2,1)S(1)} %reshape.113), channel_id=1, replica_groups=mesh['seq'=8,'exp'=4] {'exp'}, dimensions={0} | all-to-all | bytes 557056 | tf_op jit(solution)/shard_map/all_to_all | solution.py:144
  694.9 54.8 %all-gather.11.cloned.1.call-done = bf16[8,34,4096]{2,1,0:T(8,128)(2,1)} async-done(((bf16[1,34,4096]{2,1,0:T(8,128)(2,1)}), bf16[8,34,4096]{2,1,0:T(8,128)(2,1)}) %all-gather.11.cloned.1.call-update) | async-done | bytes 2228240 | tf_op jit(solution)/shard_map/all_gather | solution.py:147
  751.8 7.8 fusion.12
  759.5 17.2 %fusion.14 = bf16[272,4096]{1,0:T(8,128)(2,1)} fusion(bf16[1,1536,4096]{2,1,0:T(8,128)(2,1)} %param.35, bf16[272,4096]{1,0:T(8,128)(2,1)S(1)} %reshape.119, bf16[1,4096,1536]{2,1,0:T(8,128)(2,1)} %param.34, f32[272,1536]{1,0:T(8,128)} %fusion.12), kind=kOutput, calls=%fused_computation.48 | convolution fusion | flops 6848724992 | bytes 31293440 | tf_op jit(solution)/shard_map/dot_general | solution.py:151
  776.7 55.8 %fusion = bf16[40,4096]{1,0:T(8,128)(2,1)S(1)} fusion(bf16[272,4096]{1,0:T(8,128)(2,1)} %fusion.14), kind=kCustom, calls=%all-reduce-scatter | all-reduce-scatter fusion | flops 1310721 | bytes 2556416
  845.1 22.4 %reduce = bf16[4096,34]{1,0:T(8,128)(2,1)S(1)} reduce(bf16[4096,1,34]{2,1,0:T(2,128)(2,1)S(1)} %bitcast.86, bf16[]{:T(256)} %broadcast.100), dimensions={1}, to_apply=%bitcast.67.reduce_sub_computation | reduce | bytes 557058
  869.7 10.8 %all_to_all.31 = bf16[4,2,17408]{2,1,0:T(2,128)(2,1)S(1)} all-to-all(bf16[4,2,17408]{2,1,0:T(2,128)(2,1)S(1)} %reshape.124), channel_id=1, replica_groups=mesh['seq'=8,'exp'=4] {'exp'}, dimensions={0} | all-to-all | bytes 557056 | tf_op jit(solution)/shard_map/all_to_all | solution.py:156
  884.3 4.8 copy.75
  (346 shorter events, 282.5 us)
Async XLA Ops:
  6.5 8.0 copy-start
  6.5 42.3 %all-reduce.20.cloned.1.call-start = ((), (), s32[]{:S(2)}) async-start(), calls=%async_computation.3 | async-start | bytes 327680 | tf_op jit(solution)/shard_map/psum | solution.py:80
  7.5 4.1 collective-permute-start
  11.5 4.5 copy-start.19
  11.5 4.5 copy-start.21
  11.6 4.5 copy-start.23
  14.5 35.8 %copy-start.27 = (f32[2048]{0:T(1024)S(1)}, f32[2048]{0:T(1024)}, u32[]{:S(2)}) copy-start(f32[2048]{0:T(1024)} %param.25) | copy-start | bytes 24580
  16.0 399.5 %all-gather.9.cloned.1.call-start = ((), (), s32[]{:S(2)}) async-start(), calls=%async_computation.6 | async-start | bytes 1179648 | tf_op jit(solution)/shard_map/all_gather | solution.py:95
  58.2 14.7 %copy-start.4 = (f32[8,2048,16]{1,2,0:T(8,128)}, f32[8,2048,16]{1,2,0:T(8,128)S(1)}, u32[]{:S(2)}) copy-start(f32[8,2048,16]{1,2,0:T(8,128)S(1)} %get-tuple-element.179) | copy-start | bytes 3145732 | tf_op jit(solution)/shard_map/while
  125.2 4.1 copy-start.3
  129.3 5.5 copy-start.11
  129.3 5.5 copy-start.16
  138.1 14.7 %copy-start.4 = (f32[8,2048,16]{1,2,0:T(8,128)}, f32[8,2048,16]{1,2,0:T(8,128)S(1)}, u32[]{:S(2)}) copy-start(f32[8,2048,16]{1,2,0:T(8,128)S(1)} %get-tuple-element.179) | copy-start | bytes 3145732 | tf_op jit(solution)/shard_map/while
  209.1 5.4 copy-start.11
  209.1 5.4 copy-start.16
  217.9 14.7 %copy-start.4 = (f32[8,2048,16]{1,2,0:T(8,128)}, f32[8,2048,16]{1,2,0:T(8,128)S(1)}, u32[]{:S(2)}) copy-start(f32[8,2048,16]{1,2,0:T(8,128)S(1)} %get-tuple-element.179) | copy-start | bytes 3145732 | tf_op jit(solution)/shard_map/while
  289.0 5.5 copy-start.11
  289.0 5.5 copy-start.16
  297.8 14.7 %copy-start.4 = (f32[8,2048,16]{1,2,0:T(8,128)}, f32[8,2048,16]{1,2,0:T(8,128)S(1)}, u32[]{:S(2)}) copy-start(f32[8,2048,16]{1,2,0:T(8,128)S(1)} %get-tuple-element.179) | copy-start | bytes 3145732 | tf_op jit(solution)/shard_map/while
  368.8 5.5 copy-start.11
  368.8 5.5 copy-start.16
  374.3 270.6 %all-gather.7.cloned.1.call-start = ((), (), s32[]{:S(2)}) async-start(), calls=%async_computation.4 | async-start | bytes 18874368 | tf_op jit(solution)/shard_map/all_gather | solution.py:113
  375.0 302.3 %reduce-scatter.4.cloned.1.call-start = ((), (), s32[]{:S(2)}) async-start(), calls=%async_computation.5 | async-start | bytes 1310720 | tf_op jit(solution)/shard_map/reduce_scatter | solution.py:116
  376.6 41.2 %copy-start.14 = (f32[4,16,16]{2,1,0:T(8,128)S(1)}, f32[4,16,16]{2,1,0:T(8,128)}, u32[]{:S(2)}) copy-start(f32[4,16,16]{2,1,0:T(8,128)} %get-tuple-element.251) | copy-start | bytes 12292
  421.4 233.3 %copy-start.29 = (s32[64,2]{0,1:T(2,128)S(1)}, s32[64,2]{0,1:T(2,128)}, u32[]{:S(2)}) copy-start(s32[64,2]{0,1:T(2,128)} %param.31) | copy-start | bytes 1540
  421.4 255.9 %copy-start.17 = (bf16[64,1024]{1,0:T(8,128)(2,1)S(1)}, bf16[64,1024]{1,0:T(8,128)(2,1)}, u32[]{:S(2)}) copy-start(bf16[64,1024]{1,0:T(8,128)(2,1)} %param.29) | copy-start | bytes 393220
  654.7 95.0 %all-gather.11.cloned.1.call-start = ((), (), s32[]{:S(2)}) async-start(), calls=%async_computation.7 | async-start | bytes 2949120 | tf_op jit(solution)/shard_map/all_gather | solution.py:147
  776.7 60.4 %copy-start.30 = (u32[32]{0:T(128)S(1)}, u32[32]{0:T(128)}, u32[]{:S(2)}) copy-start(u32[32]{0:T(128)} %constant.108) | copy-start | bytes 388
  832.6 8.2 collective-permute-start.1
  835.5 2.8 collective-permute-start.2
  884.3 6.2 copy-start.1
  884.3 5.2 copy-start.31
  (42 other events, 100.2 us)
Sparse Core Ops, SparseCore 0:
  16.2 32.5 all-reduce.19
  374.4 41.0 all-gather.8
  417.8 227.0 all-gather.6
  654.8 22.4 reduce-scatter.3
  695.0 54.6 all-gather.10
where the time goes:
time: 905 us; the launch traced here: 897 us
  waiting for transfers between devices  349 us (39%)
  local copies, waits for them, and re-layouts  230 us (25%)
  other arithmetic  148 us (16%)
  blocking collectives  106 us (12%)
  matrix products  40.7 us (4%)
  between operations  14.3 us (2%)
    all_gather x1, waiting for transfers between devices, per_device(): lax.all_gather(out_proj, 'seq', axis=1, tiled=True)  223 us
    pad x48, local copies, waits for them, and re-layouts, advance(): products, sums = lax.associative_scan(combine_pairs, (decay, drive), axis=0)  178 us
    unnamed x1, blocking collectives  55.8 us
    all_gather x1, waiting for transfers between devices, per_device(): lax.all_gather(arrived, 'seq', axis=0, tiled=True)  54.8 us
    add x24, other arithmetic, advance(): products, sums = lax.associative_scan(combine_pairs, (decay, drive), axis=0)  45.8 us
    psum x1, waiting for transfers between devices, per_device(): projected = lax.psum(partial_proj, 'exp')  32.7 us
    add x20, other arithmetic, combine_pairs(): return (earlier[0] * later[0], later[0] * earlier[1] + later[1])  25 us
    all_gather x1, blocking collectives, per_device(): lax.all_gather(size_total[None], 'seq', axis=0, tiled=True)  24.4 us
  transfers between devices with their start and end apart: 8, of which 6 were waited for; matrix products, arithmetic and copies ran while one was open for 1% of the time, Pallas kernels for 0%

commit v1 on v0

v1 whole, which is shorter than its diff:
```python
import functools
import math

import jax
import jax.numpy as jnp
from jax import lax
from jax.experimental import pallas as pl
from jax.experimental.pallas import tpu as pltpu
from jax.sharding import PartitionSpec as P

eps = 1e-05
LOG2E = 1.4426950408889634
MIB = 1 << 20


def tile_of(size, most=512):
    return max(t for t in range(128, most + 1, 128) if size % t == 0)


def whole_vmem():
    return pl.BlockSpec(memory_space=pltpu.VMEM)


def whole_smem():
    return pl.BlockSpec(memory_space=pltpu.SMEM)


def conv_kernel(x_ref, halo_ref, weight_ref, bias_ref, proj_ref, xconv_ref, partial_ref):
    rows = x_ref.shape[0]
    taps = weight_ref.shape[0]
    extended = jnp.concatenate(
        [halo_ref[...].astype(jnp.float32), x_ref[...].astype(jnp.float32)], axis=0
    )
    pad = halo_ref.shape[0]
    conv = jnp.zeros(x_ref.shape, jnp.float32) + bias_ref[...]
    for tap in range(taps):
        start = pad - (taps - 1) + tap
        conv = conv + weight_ref[tap : tap + 1, :] * extended[start : start + rows]
    xconv = (conv / (1.0 + jnp.exp(-conv))).astype(jnp.bfloat16)
    xconv_ref[...] = xconv

    @pl.when(pl.program_id(0) == 0)
    def _():
        partial_ref[...] = jnp.zeros_like(partial_ref)

    partial_ref[...] += jnp.dot(xconv, proj_ref[...], preferred_element_type=jnp.float32)


def conv_and_project(x_in, halo, conv_weight, conv_bias, x_proj):
    rows, channels = x_in.shape
    width = tile_of(channels)
    columns = x_proj.shape[1]
    return pl.pallas_call(
        conv_kernel,
        grid=(channels // width,),
        in_specs=[
            pl.BlockSpec((rows, width), lambda i: (0, i)),
            pl.BlockSpec((halo.shape[0], width), lambda i: (0, i)),
            pl.BlockSpec((conv_weight.shape[0], width), lambda i: (0, i)),
            pl.BlockSpec((1, width), lambda i: (0, i)),
            pl.BlockSpec((width, columns), lambda i: (i, 0)),
        ],
        out_specs=[
            pl.BlockSpec((rows, width), lambda i: (0, i)),
            pl.BlockSpec((rows, columns), lambda i: (0, 0)),
        ],
        out_shape=[
            jax.ShapeDtypeStruct((rows, channels), jnp.bfloat16),
            jax.ShapeDtypeStruct((rows, columns), jnp.float32),
        ],
        name="conv_project",
    )(x_in, halo, conv_weight, conv_bias, x_proj)


def softplus(v):
    return jnp.maximum(v, 0.0) + jnp.log1p(jnp.exp(-jnp.abs(v)))


def ends_kernel(low_ref, proj_ref, bias_ref, rate_ref, x_ref, b_ref, size_ref, load_ref, drive_ref):
    rows, width = x_ref.shape
    states = rate_ref.shape[0]
    groups = width // 128
    size = softplus(
        jnp.dot(low_ref[...], proj_ref[...], preferred_element_type=jnp.float32) + bias_ref[...]
    )
    size_ref[...] = size
    drive_ref[...] = size * x_ref[...].astype(jnp.float32)
    rates = rate_ref[...]

    def step(block, state):
        start = pl.multiple_of(block * 8, 8)
        sizes = size_ref[pl.ds(start, 8), :]
        drives = drive_ref[pl.ds(start, 8), :]
        state = list(state)
        for i in range(8):
            b_now = b_ref[start + i]
            for g in range(groups):
                lanes = slice(g * 128, g * 128 + 128)
                decay = jnp.exp2(sizes[i : i + 1, lanes] * rates[:, lanes])
                state[g] = decay * state[g] + drives[i : i + 1, lanes] * b_now
        return tuple(state)

    zero = jnp.zeros((states, 128), jnp.float32)
    state = lax.fori_loop(0, rows // 8, step, (zero,) * groups)
    total = jnp.sum(size, axis=0, keepdims=True)
    high = total.astype(jnp.bfloat16).astype(jnp.float32)
    low = total - high
    rest = jnp.zeros((load_ref.shape[0] - states - 2, width), jnp.float32)
    load_ref[...] = jnp.concatenate(
        [jnp.concatenate(state, axis=1), high, low, rest], axis=0
    ).astype(jnp.bfloat16)


def scan_ends(dt_low, dt_proj, dt_bias, rates, xconv, b_wide):
    rows, channels = xconv.shape
    states = rates.shape[0]
    width = tile_of(channels)
    load_rows = -(-(states + 2) // 16) * 16
    return pl.pallas_call(
        ends_kernel,
        grid=(channels // width,),
        in_specs=[
            pl.BlockSpec(dt_low.shape, lambda i: (0, 0)),
            pl.BlockSpec((dt_proj.shape[0], width), lambda i: (0, i)),
            pl.BlockSpec((1, width), lambda i: (0, i)),
            pl.BlockSpec((states, width), lambda i: (0, i)),
            pl.BlockSpec((rows, width), lambda i: (0, i)),
            pl.BlockSpec(b_wide.shape, lambda i: (0, 0, 0)),
        ],
        out_specs=[
            pl.BlockSpec((rows, width), lambda i: (0, i)),
            pl.BlockSpec((load_rows, width), lambda i: (0, i)),
        ],
        out_shape=[
            jax.ShapeDtypeStruct((rows, channels), jnp.float32),
            jax.ShapeDtypeStruct((load_rows, channels), jnp.bfloat16),
        ],
        scratch_shapes=[pltpu.VMEM((rows, width), jnp.float32)],
        name="scan_ends",
    )(dt_low, dt_proj, dt_bias, rates, xconv, b_wide)


def mix_kernel(
    place_ref, load_ref, size_ref, x_ref, z_ref, b_ref, c_ref, rate_ref, skip_ref, out_ref, drive_ref, y_ref
):
    rows, width = x_ref.shape
    states = rate_ref.shape[0]
    groups = width // 128
    rates = rate_ref[...]
    x_f = x_ref[...].astype(jnp.float32)
    drive_ref[...] = size_ref[...] * x_f

    def earlier(j, state):
        block = load_ref[j].astype(jnp.float32)
        total = block[states : states + 1] + block[states + 1 : states + 2]
        return jnp.exp2(total * rates) * state + block[:states]

    incoming = lax.fori_loop(0, place_ref[0], earlier, jnp.zeros((states, width), jnp.float32))

    def step(block, state):
        start = pl.multiple_of(block * 8, 8)
        sizes = size_ref[pl.ds(start, 8), :]
        drives = drive_ref[pl.ds(start, 8), :]
        state = list(state)
        outs = [[None] * 8 for _ in range(groups)]
        for i in range(8):
            b_now = b_ref[start + i]
            c_now = c_ref[start + i]
            for g in range(groups):
                lanes = slice(g * 128, g * 128 + 128)
                decay = jnp.exp2(sizes[i : i + 1, lanes] * rates[:, lanes])
                state[g] = decay * state[g] + drives[i : i + 1, lanes] * b_now
                outs[g][i] = jnp.sum(state[g] * c_now, axis=0, keepdims=True)
        for g in range(groups):
            y_ref[pl.ds(start, 8), g * 128 : g * 128 + 128] = jnp.concatenate(outs[g], axis=0)
        return tuple(state)

    start_state = tuple(incoming[:, g * 128 : g * 128 + 128] for g in range(groups))
    lax.fori_loop(0, rows // 8, step, start_state)
    z_f = z_ref[...].astype(jnp.float32)
    scanned = y_ref[...] + skip_ref[...] * x_f
    out_ref[...] = (scanned * (z_f / (1.0 + jnp.exp(-z_f)))).astype(jnp.bfloat16)


def scan_mix(place, loads, step_size, xconv, z_in, b_wide, c_wide, rates, d_skip):
    rows, channels = xconv.shape
    states = rates.shape[0]
    width = tile_of(channels)

    def by_lane(depth):
        return pl.BlockSpec((depth, width), lambda i: (0, i))

    return pl.pallas_call(
        mix_kernel,
        grid=(channels // width,),
        in_specs=[
            whole_smem(),
            pl.BlockSpec((loads.shape[0], loads.shape[1], width), lambda i: (0, 0, i)),
            by_lane(rows),
            by_lane(rows),
            by_lane(rows),
            pl.BlockSpec(b_wide.shape, lambda i: (0, 0, 0)),
            pl.BlockSpec(c_wide.shape, lambda i: (0, 0, 0)),
            by_lane(states),
            by_lane(1),
        ],
        out_specs=by_lane(rows),
        out_shape=jax.ShapeDtypeStruct((rows, channels), jnp.bfloat16),
        scratch_shapes=[pltpu.VMEM((rows, width), jnp.float32)] * 2,
        name="scan_mix",
    )(place, loads, step_size, xconv, z_in, b_wide, c_wide, rates, d_skip)


def out_kernel(count, order_ref, *refs):
    blocks, weight_ref, out_ref, held_ref = refs[:count], refs[count], refs[count + 1], refs[count + 2]
    rows = blocks[0].shape[0]
    for i in range(count):
        held_ref[pl.ds(pl.multiple_of(order_ref[i] * rows, rows), rows), :] = blocks[i][...]
    out_ref[...] = jnp.dot(
        held_ref[...], weight_ref[...], preferred_element_type=jnp.float32
    ).astype(jnp.bfloat16)


def out_product(order, blocks, weight):
    rows, depth = blocks[0].shape
    count = len(blocks)
    return pl.pallas_call(
        functools.partial(out_kernel, count),
        in_specs=[whole_smem()] + [whole_vmem()] * (count + 1),
        out_specs=whole_vmem(),
        out_shape=jax.ShapeDtypeStruct((count * rows, weight.shape[1]), jnp.bfloat16),
        scratch_shapes=[pltpu.VMEM((count * rows, depth), jnp.bfloat16)],
        compiler_params=pltpu.CompilerParams(vmem_limit_bytes=32 * MIB),
        name="out_product",
    )(order, *blocks, weight)


def hidden_kernel(count, order_ref, place_ref, *refs):
    chunks = refs[:count]
    gain_ref, gate_ref, up_ref, act_ref, own_ref, h_ref, gate_sum, up_sum, squares = refs[count:]
    step = pl.program_id(0)
    rows, depth = h_ref.shape
    columns = gate_sum.shape[1]
    width = tile_of(columns)
    own_rows = own_ref.shape[0]
    for i in range(count):

        @pl.when(step == i)
        def _(i=i):
            h_ref[...] = chunks[i][...].astype(jnp.float32)

    @pl.when(step == 0)
    def _():
        gate_sum[...] = jnp.zeros_like(gate_sum)
        up_sum[...] = jnp.zeros_like(up_sum)
        squares[...] = jnp.zeros_like(squares)

    own_ref[...] = h_ref[pl.ds(pl.multiple_of(place_ref[0] * own_rows, own_rows), own_rows), :]
    h = h_ref[...]
    squares[...] += jnp.sum(h * h, axis=1, keepdims=True)
    scaled = (h * gain_ref[0]).astype(jnp.bfloat16)
    for start in range(0, columns, width):
        at = slice(start, start + width)
        gate_sum[:, at] += jnp.dot(scaled, gate_ref[0, :, at], preferred_element_type=jnp.float32)
        up_sum[:, at] += jnp.dot(scaled, up_ref[0, :, at], preferred_element_type=jnp.float32)

    @pl.when(step == count - 1)
    def _():
        scale = lax.rsqrt(squares[...] / (depth * count) + eps)
        for start in range(0, columns, width):
            at = slice(start, start + width)
            gate = gate_sum[:, at] * scale
            upper = up_sum[:, at] * scale
            act_ref[:, at] = (gate / (1.0 + jnp.exp(-gate)) * upper).astype(jnp.bfloat16)


def expert_hidden(order, place, chunks, gain, w_gate, w_up, own_rows):
    rows, depth = chunks[0].shape
    count = len(chunks)
    columns = w_gate.shape[2]
    gain = gain.reshape(count, 1, depth)
    weight_spec = pl.BlockSpec((1, depth, columns), lambda k, order, place: (0, order[k], 0))
    return pl.pallas_call(
        functools.partial(hidden_kernel, count),
        grid_spec=pltpu.PrefetchScalarGridSpec(
            num_scalar_prefetch=2,
            grid=(count,),
            in_specs=[whole_vmem()] * count
            + [
                pl.BlockSpec((1, 1, depth), lambda k, order, place: (order[k], 0, 0)),
                weight_spec,
                weight_spec,
            ],
            out_specs=[
                pl.BlockSpec((rows, columns), lambda k, order, place: (0, 0)),
                pl.BlockSpec((own_rows, depth), lambda k, order, place: (0, order[k])),
            ],
            scratch_shapes=[
                pltpu.VMEM((rows, depth), jnp.float32),
                pltpu.VMEM((rows, columns), jnp.float32),
                pltpu.VMEM((rows, columns), jnp.float32),
                pltpu.VMEM((rows, 1), jnp.float32),
            ],
        ),
        out_shape=[
            jax.ShapeDtypeStruct((rows, columns), jnp.bfloat16),
            jax.ShapeDtypeStruct((own_rows, depth * count), jnp.float32),
        ],
        compiler_params=pltpu.CompilerParams(vmem_limit_bytes=40 * MIB),
        name="expert_hidden",
    )(order, place, *chunks, gain, w_gate, w_up)


def down_kernel(z_count, x_count, z_ref, x_ref, act_ref, weight_ref, *refs):
    outs, held_ref = refs[:-1], refs[-1]
    held_ref[...] = jnp.dot(act_ref[...], weight_ref[0], preferred_element_type=jnp.float32)
    pitch = outs[0].shape[0]
    for r in range(z_count):
        for i in range(x_count):
            block = lax.rem(z_ref[0] + r, z_count) * x_count + lax.rem(x_ref[0] + i, x_count)
            start = pl.multiple_of(block * pitch, pitch)
            outs[r * x_count + i][...] = held_ref[pl.ds(start, pitch), :].astype(jnp.bfloat16)


def expert_down(z_at, x_at, z_count, x_count, act, w_down):
    rows, depth = act.shape
    columns = w_down.shape[2]
    width = tile_of(columns)
    blocks = z_count * x_count
    pitch = rows // blocks
    outs = pl.pallas_call(
        functools.partial(down_kernel, z_count, x_count),
        grid_spec=pltpu.PrefetchScalarGridSpec(
            num_scalar_prefetch=2,
            grid=(columns // width,),
            in_specs=[
                pl.BlockSpec((rows, depth), lambda n, z, x: (0, 0)),
                pl.BlockSpec((1, depth, width), lambda n, z, x: (0, 0, n)),
            ],
            out_specs=[pl.BlockSpec((pitch, width), lambda n, z, x: (0, n))] * blocks,
            scratch_shapes=[pltpu.VMEM((rows, width), jnp.float32)],
        ),
        out_shape=[jax.ShapeDtypeStruct((pitch, columns), jnp.bfloat16)] * blocks,
        compiler_params=pltpu.CompilerParams(vmem_limit_bytes=32 * MIB),
        name="expert_down",
    )(z_at, x_at, act, w_down)
    return [outs[r * x_count : (r + 1) * x_count] for r in range(z_count)]


def per_device(
    x_in,
    z_in,
    conv_weight,
    conv_bias,
    x_proj,
    dt_proj,
    dt_bias,
    a_log,
    d_skip,
    out_proj,
    resid,
    norm_gain,
    routes,
    route_gate,
    w_gate,
    w_up,
    w_down,
):
    row_count, channels = x_in.shape
    seq_count = lax.axis_size("seq")
    exp_count = lax.axis_size("exp")
    x_count = seq_count // exp_count
    z_count = exp_count
    seq_at = lax.axis_index("seq")
    exp_at = lax.axis_index("exp")
    z_at, x_at = seq_at // x_count, seq_at % x_count
    z_one, x_one = z_at.reshape(1).astype(jnp.int32), x_at.reshape(1).astype(jnp.int32)
    seq_one = seq_at.reshape(1).astype(jnp.int32)
    top_count = routes.shape[1]
    capacity = row_count * top_count * 17 // (16 * exp_count)
    pitch = -(-capacity // 8) * 8
    group_tokens = x_count * row_count
    feature_slice = resid.shape[1]
    column_slice = out_proj.shape[1]

    def from_z(block, r):
        pairs = [
            (((z + r) % z_count) * x_count + x, z * x_count + x)
            for z in range(z_count)
            for x in range(x_count)
        ]
        return lax.ppermute(block, "seq", pairs)

    def from_x(block, i):
        pairs = [
            (z * x_count + (x + i) % x_count, z * x_count + x)
            for z in range(z_count)
            for x in range(x_count)
        ]
        return lax.ppermute(block, "seq", pairs)

    def gathered(block):
        along_z = [block] + [from_z(block, r) for r in range(1, z_count)]
        return [
            held if i == 0 else from_x(held, i) for held in along_z for i in range(x_count)
        ]

    order = jnp.stack(
        [
            ((z_at + r) % z_count) * x_count + (x_at + i) % x_count
            for r in range(z_count)
            for i in range(x_count)
        ]
    ).astype(jnp.int32)

    halo = lax.ppermute(
        x_in[row_count - 8 :], "seq", [(i, i + 1) for i in range(seq_count - 1)]
    )
    routes_all = lax.all_gather(routes, "seq", axis=0, tiled=True)

    resid_parts = []
    resid_cut = resid.reshape(row_count, x_count, column_slice)
    for k in range(x_count):
        piece = lax.dynamic_index_in_dim(resid_cut, (x_at - k) % x_count, 1, keepdims=False)
        pairs = []
        for s in range(seq_count):
            for e in range(exp_count):
                source_s = x_count * e + (s % x_count + k) % x_count
                pairs.append((source_s * exp_count + s // x_count, s * exp_count + e))
        resid_parts.append(lax.ppermute(piece, ("seq", "exp"), pairs))
    resid_stack = jnp.stack(resid_parts + resid_parts)
    resid_here = lax.dynamic_slice_in_dim(
        resid_stack, (x_count - x_at) % x_count, x_count, 0
    ).reshape(group_tokens, column_slice)

    def slots_of(named):
        flat = named.reshape(-1, row_count * top_count)
        onehot = (flat[:, :, None] == jnp.arange(exp_count, dtype=jnp.int32)).astype(jnp.float32)
        below = jnp.tril(jnp.ones((row_count * top_count,) * 2, jnp.float32), -1)
        counts = jnp.einsum("ij,bje->bie", below, onehot)
        slots = jnp.sum(counts * onehot, axis=2).astype(jnp.int32)
        return slots.reshape(-1, row_count, top_count)

    group_routes = lax.dynamic_slice_in_dim(routes_all, exp_at * group_tokens, group_tokens, 0)
    group_routes = group_routes.reshape(x_count, row_count, top_count)
    target = (
        group_routes * (x_count * pitch)
        + jnp.arange(x_count, dtype=jnp.int32)[:, None, None] * pitch
        + slots_of(group_routes)
    ).reshape(group_tokens, top_count)
    slot_ids = jnp.arange(exp_count * x_count * pitch, dtype=jnp.int32)
    dispatch = jnp.sum(
        (target[None, :, :] == slot_ids[:, None, None]).astype(jnp.float32), axis=2
    ).astype(jnp.bfloat16)

    own_slots = slots_of(routes)[0]
    at_slot = (routes == exp_at)[None] & (
        own_slots[None] == jnp.arange(pitch, dtype=jnp.int32)[:, None, None]
    )
    gate_here = jnp.sum(jnp.where(at_slot, route_gate[None], 0.0), axis=(1, 2))[:, None]
    first_here = jnp.sum(at_slot[:, :, 0].astype(jnp.float32), axis=1)[:, None]
    own_target = routes * pitch + own_slots
    back_ids = jnp.arange(exp_count * pitch, dtype=jnp.int32)
    choose = jnp.sum(
        (own_target[:, :, None] == back_ids[None, None, :]).astype(jnp.float32), axis=1
    ).astype(jnp.bfloat16)

    rates = -jnp.exp(a_log.T) * LOG2E
    xconv, partial = conv_and_project(x_in, halo, conv_weight, conv_bias[None], x_proj)
    partials = lax.all_to_all(
        jnp.broadcast_to(partial[None], (exp_count,) + partial.shape), "exp", 0, 0, tiled=True
    )
    projected = jnp.sum(partials, axis=0)
    low_rank = dt_proj.shape[0]
    state_count = a_log.shape[1]
    dt_low = projected[:, :low_rank].astype(jnp.bfloat16)
    b_mat = projected[:, low_rank : low_rank + state_count]
    c_mat = projected[:, low_rank + state_count :]
    b_wide = jnp.broadcast_to(b_mat[:, :, None], b_mat.shape + (128,))
    c_wide = jnp.broadcast_to(c_mat[:, :, None], c_mat.shape + (128,))
    step_size, load = scan_ends(dt_low, dt_proj, dt_bias[None], rates, xconv, b_wide)
    loads = lax.all_to_all(
        jnp.broadcast_to(load[None], (seq_count,) + load.shape), "seq", 0, 0, tiled=True
    )
    mixed = scan_mix(
        seq_one, loads, step_size, xconv, z_in, b_wide, c_wide, rates, d_skip[None]
    )
    partial_out = out_product(order, gathered(mixed), out_proj)
    arrived = lax.all_to_all(
        partial_out.reshape(exp_count, group_tokens, column_slice), "exp", 0, 0, tiled=True
    )
    mamba_out = jnp.sum(arrived.astype(jnp.float32), axis=0)
    hidden_state = (resid_here.astype(jnp.float32) + mamba_out).astype(jnp.bfloat16)

    outgoing = jnp.dot(dispatch, hidden_state, preferred_element_type=jnp.float32)
    outgoing = outgoing.astype(jnp.bfloat16).reshape(exp_count, x_count * pitch, column_slice)
    rows_here = lax.all_to_all(outgoing, "exp", 0, 0, tiled=True)
    rows_here = rows_here.reshape(exp_count * x_count * pitch, column_slice)
    act, own_hidden = expert_hidden(
        order, seq_one, gathered(rows_here), norm_gain, w_gate, w_up, pitch
    )
    down = expert_down(z_one, x_one, z_count, x_count, act, w_down)

    def over_x(r):
        pieces = [down[r][0]] + [
            from_x(down[r][i], x_count - i) for i in range(1, x_count)
        ]
        return functools.reduce(jnp.add, [p.astype(jnp.float32) for p in pieces])

    total = over_x(0)
    for r in range(1, z_count):
        sent = from_z(over_x(r).astype(jnp.bfloat16), z_count - r)
        total = total + sent.astype(jnp.float32)
    expert_out = total.astype(jnp.bfloat16).astype(jnp.float32)
    weighted = (gate_here * expert_out + first_here * own_hidden).astype(jnp.bfloat16)
    weighted = weighted.reshape(pitch, exp_count, feature_slice).transpose(1, 0, 2)
    back = lax.all_to_all(weighted, "exp", 0, 0, tiled=True)
    back = back.reshape(exp_count * pitch, feature_slice)
    return jnp.dot(choose, back, preferred_element_type=jnp.float32).astype(jnp.bfloat16)


def solution(mesh):
    return jax.shard_map(
        per_device,
        mesh=mesh,
        in_specs=(
            P("seq", "exp"),
            P("seq", "exp"),
            P(None, "exp"),
            P("exp"),
            P("exp", None),
            P(None, "exp"),
            P("exp"),
            P("exp", None),
            P("exp"),
            P("exp", "seq"),
            P("seq", "exp"),
            P(),
            P("seq", None),
            P("seq", None),
            P("exp", None, "seq"),
            P("exp", None, "seq"),
            P("exp", "seq", None),
        ),
        out_specs=P("seq", "exp"),
        check_vma=False,
    )
```

time: 905 us -> 283 us (0.31)
  waiting for transfers between devices: 349 us -> 113 us
  local copies, waits for them, and re-layouts: 230 us -> 17 us
  other arithmetic: 148 us -> 3.7 us
  blocking collectives: 106 us -> 30.8 us
  starting transfers between devices: 7.73 us -> 68.9 us
  Pallas kernels: 0 us -> 43.2 us
  matrix products: 40.7 us -> 1.55 us
  between operations: 14.3 us -> 0.34 us
    all_gather x3 -> x0, waiting for transfers between devices: 293 us -> none  [the longest x1 223 us: per_device(): lax.all_gather(out_proj, 'seq', axis=1, tiled=True)]
    pad x48 -> x0, local copies, waits for them, and re-layouts: 178 us -> none  [advance(): products, sums = lax.associative_scan(combine_pairs, (decay, drive), axis=0)]
    add x45 -> x3, other arithmetic: 70.8 us -> 0.01 us  [the longest x1 0.01 us: per_device(): group_routes * (x_count * pitch)]
    ppermute x1 -> x24, waiting for transfers between devices: 0.01 us -> 69.6 us  [the longest x12 40.7 us: from_x(): return lax.ppermute(block, 'seq', pairs)]
    unnamed x1 -> x0, blocking collectives: 55.8 us -> none
    all_to_all x0 -> x4, waiting for transfers between devices: none -> 43.2 us  [the longest x1 25 us: per_device(): lax.all_to_all(jnp.broadcast_to(load[None], (seq_count,) + load.shape), '...]
    pallas_call x0 -> x6, Pallas kernels: none -> 43.2 us  [the longest x1 17.4 us: expert_hidden(): pl.pallas_call(functools.partial(hidden_kernel, count), grid_spec=pltpu.P...]
    dot_general x7 -> x4, matrix products: 40.7 us -> 1.55 us  [the longest x1 0.84 us: per_device(): jnp.dot(choose, back, preferred_element_type=jnp.float32)]
  transfers between devices with their start and end apart: 8 -> 28, of which waited for: 6 -> 16; matrix products, arithmetic and copies ran while one was open for 1% -> 4% of each run, Pallas kernels for 0% -> 1%
where the time goes in v1:
time: 283 us; the launch traced here: 278 us
  waiting for transfers between devices  113 us (40%)
  starting transfers between devices  68.9 us (24%)
  Pallas kernels  43.2 us (15%)
  blocking collectives  30.8 us (11%)
  local copies, waits for them, and re-layouts  17 us (6%)
  other arithmetic  3.7 us (1%)
    ppermute x12, waiting for transfers between devices, from_x(): return lax.ppermute(block, 'seq', pairs)  40.7 us
    ppermute x9, waiting for transfers between devices, from_z(): return lax.ppermute(block, 'seq', pairs)  28.8 us
    all_to_all x1, waiting for transfers between devices, per_device(): lax.all_to_all(jnp.broadcast_to(load[None], (seq_count,) + load.shape), '...  25 us
    all_gather x1, blocking collectives, per_device(): routes_all = lax.all_gather(routes, 'seq', axis=0, tiled=True)  21.9 us
    ppermute x2, starting transfers between devices, per_device(): resid_parts.append(lax.ppermute(piece, ('seq', 'exp'), pairs))  17.4 us
    pallas_call x1, Pallas kernels, expert_hidden(): pl.pallas_call(functools.partial(hidden_kernel, count), grid_spec=pltpu.P...  17.4 us
    all_to_all x1, starting transfers between devices, per_device(): lax.all_to_all(partial_out.reshape(exp_count, group_tokens, column_slice)...  12 us
    ppermute x12, starting transfers between devices, from_x(): return lax.ppermute(block, 'seq', pairs)  10.5 us
  transfers between devices with their start and end apart: 28, of which 16 were waited for; matrix products, arithmetic and copies ran while one was open for 4% of the time, Pallas kernels for 1%

profile of v1, /device:TPU:5, one launch (start us, length us, event | category | flops | bytes accessed | tf_op | source)
XLA Modules:
  0.0 278.2 jit_solution(14195136271994532961)
XLA Ops:
  0.8 3.1 %collective-permute-start.2 = (bf16[8,2048]{1,0:T(8,128)(2,1)S(1)}, bf16[8,2048]{1,0:T(8,128)(2,1)S(1)}, u32[]{:S(2)}, u32[]{:S(2)}) collective-permute-start(bf16[8,2048]{1,0:T(8,128)(2,1)S(1)} %slice.16), channel_id=1, source_target_pairs={{0,4},{4,8},{8,12},{12,16},{16,20},{20,24},{24,28},{1,5},{5,9},{9,... | collective-permute-start | bytes 98312 | tf_op jit(solution)/shard_map/ppermute | solution.py:416
  3.9 4.3 %copy.73.proj_ref = bf16[2048,544]{1,0:T(8,128)(2,1)} copy(bf16[2048,544]{0,1:T(8,128)(2,1)} %param.21) | data formatting | bytes 4456448 | tf_op args[4]
  8.8 4.3 %conv_project.1 = (bf16[64,2048]{1,0:T(8,128)(2,1)}, f32[64,544]{1,0:T(8,128)}) custom-call(bf16[64,2048]{1,0:T(8,128)(2,1)} %x_ref.1, bf16[8,2048]{1,0:T(8,128)(2,1)} %copy-done.6, f32[4,2048]{1,0:T(4,128)} %weight_ref.2, f32[1,2048]{1,0:T(1,128)} %bitcast.76, bf16[2048,544]{1,0:T(8,128)(2,1)} %copy.73.proj_ref), custom_call_target="tpu_custom_call" | custom-call | tf_op jit(solution)/shard_map/conv_project/pallas_call | solution.py:53
  14.9 4.6 %all-to-all-start = ((f32[4,64,544]{2,1,0:T(8,128)}), f32[4,64,544]{2,1,0:T(8,128)S(1)}, u32[]{:S(2)}, u32[]{:S(2)}) async-start(f32[4,64,544]{2,1,0:T(8,128)} %broadcast_in_dim.35), calls=%async_computation | async-start | bytes 1310720 | tf_op jit(solution)/shard_map/all_to_all | solution.py:470
  20.1 7.7 %all-to-all-done = f32[4,64,544]{2,1,0:T(8,128)S(1)} async-done(((f32[4,64,544]{2,1,0:T(8,128)}), f32[4,64,544]{2,1,0:T(8,128)S(1)}, u32[]{:S(2)}, u32[]{:S(2)}) %all-to-all-start) | async-done | bytes 557088 | tf_op jit(solution)/shard_map/all_to_all | solution.py:470
  29.5 5.3 %scan_ends.1 = (f32[64,2048]{1,0:T(8,128)}, bf16[32,2048]{1,0:T(8,128)(2,1)}) custom-call(bf16[64,512]{1,0:T(8,128)(2,1)} %slice.27.low_ref, bf16[512,2048]{1,0:T(8,128)(2,1)} %proj_ref.2, f32[1,2048]{1,0:T(1,128)} %bitcast.77, f32[16,2048]{1,0:T(8,128)} %multiply_bitcast_fusion.rate_ref, bf16[64,2048]{1,0:T(8,128)(2,1)} %get-tuple-element.20.x_ref, ...), custom_call_target="tpu_custom_call" | custom-call | tf_op jit(solution)/shard_map/scan_ends/pallas_call | solution.py:119
  36.8 4.6 %all-to-all-start.1 = ((bf16[8,32,2048]{2,1,0:T(8,128)(2,1)}), bf16[8,32,2048]{2,1,0:T(8,128)(2,1)S(1)}, u32[]{:S(2)}, u32[]{:S(2)}) async-start(bf16[8,32,2048]{2,1,0:T(8,128)(2,1)} %broadcast_in_dim.38), calls=%async_computation.1 | async-start | bytes 2097152 | tf_op jit(solution)/shard_map/all_to_all | solution.py:482
  41.5 25.0 %all-to-all-done.1.load_ref = bf16[8,32,2048]{2,1,0:T(8,128)(2,1)S(1)} async-done(((bf16[8,32,2048]{2,1,0:T(8,128)(2,1)}), bf16[8,32,2048]{2,1,0:T(8,128)(2,1)S(1)}, u32[]{:S(2)}, u32[]{:S(2)}) %all-to-all-start.1) | async-done | bytes 1048608 | tf_op jit(solution)/shard_map/all_to_all | solution.py:482
  67.6 6.0 %scan_mix.1.refs_0_ = bf16[64,2048]{1,0:T(8,128)(2,1)} custom-call(s32[1]{0:T(128)} %bitcast.12.place_ref, bf16[8,32,2048]{2,1,0:T(8,128)(2,1)} %copy-done.3, f32[64,2048]{1,0:T(8,128)} %get-tuple-element.22.size_ref, bf16[64,2048]{1,0:T(8,128)(2,1)} %get-tuple-element.20.x_ref, bf16[64,2048]{1,0:T(8,128)(2,1)} %z_ref.1, ...), custom_call_target="tpu_custom_call" | custom-call | tf_op jit(solution)/shard_map/scan_mix/pallas_call | solution.py:193
  73.6 2.6 collective-permute-start.4
  77.6 6.4 %collective-permute-start = (bf16[64,512]{1,0:T(8,128)(2,1)}, bf16[64,512]{1,0:T(8,128)(2,1)}, u32[]{:S(2)}, u32[]{:S(2)}) collective-permute-start(bf16[64,512]{1,0:T(8,128)(2,1)} %bitcast.60), channel_id=1, source_target_pairs={{0,0},{8,1},{16,2},{24,3},{4,4},{12,5},{20,6},{28,7},{1,8},{9,9},{... | collective-permute-start | bytes 196616 | tf_op jit(solution)/shard_map/ppermute | solution.py:430
  84.0 21.9 %all-gather = s32[8,64,2]{1,2,0:T(2,128)S(1)} all-gather(s32[1,64,2]{1,2,0:T(2,128)S(1)} %bitcast.75), channel_id=1, replica_groups=mesh['seq'=8,'exp'=4] {'seq'}, dimensions={0}, use_global_device_ids=true | all-gather | bytes 4608 | tf_op jit(solution)/shard_map/all_gather | solution.py:419
  111.5 11.0 %collective-permute-start.1 = (bf16[64,512]{1,0:T(8,128)(2,1)}, bf16[64,512]{1,0:T(8,128)(2,1)S(1)}, u32[]{:S(2)}, u32[]{:S(2)}) collective-permute-start(bf16[64,512]{1,0:T(8,128)(2,1)} %bitcast.73), channel_id=1, source_target_pairs={{4,0},{12,1},{20,2},{28,3},{0,4},{8,5},{16,6},{24,7},{5,8},{13,9},... | collective-permute-start | bytes 196616 | tf_op jit(solution)/shard_map/ppermute | solution.py:430
  122.5 4.2 %collective-permute-done.9.refs_7_ = bf16[64,2048]{1,0:T(8,128)(2,1)} collective-permute-done((bf16[64,2048]{1,0:T(8,128)(2,1)S(1)}, bf16[64,2048]{1,0:T(8,128)(2,1)}, u32[]{:S(2)}, u32[]{:S(2)}) %collective-permute-start.9) | collective-permute-done | bytes 262176 | tf_op jit(solution)/shard_map/ppermute | solution.py:400
  127.7 3.2 %out_product.1 = bf16[512,512]{1,0:T(8,128)(2,1)} custom-call(s32[8]{0:T(128)S(1)} %stack.46.order_ref, bf16[64,2048]{1,0:T(8,128)(2,1)S(1)} %copy-done.1, bf16[64,2048]{1,0:T(8,128)(2,1)S(1)} %collective-permute-done.3.refs_1_, bf16[64,2048]{1,0:T(8,128)(2,1)S(1)} %collective-permute-done.4.refs_2_, bf16[64,2048]{1,0:T(8,128)(2,1)S(1)} %collective-permute-done.5.refs_3_, ...), custom_call_target="tpu_custom_call" | custom-call | tf_op jit(solution)/shard_map/out_product/pallas_call | solution.py:227
  130.9 12.0 %all-to-all-start.2 = ((bf16[4,128,512]{2,1,0:T(8,128)(2,1)}), bf16[4,128,512]{2,1,0:T(8,128)(2,1)S(1)}, u32[]{:S(2)}, u32[]{:S(2)}) async-start(bf16[4,128,512]{2,1,0:T(8,128)(2,1)} %bitcast.23), calls=%async_computation.2 | async-start | bytes 1048576 | tf_op jit(solution)/shard_map/all_to_all | solution.py:489
  143.9 5.8 %all-to-all-done.2 = bf16[4,128,512]{2,1,0:T(8,128)(2,1)S(1)} async-done(((bf16[4,128,512]{2,1,0:T(8,128)(2,1)}), bf16[4,128,512]{2,1,0:T(8,128)(2,1)S(1)}, u32[]{:S(2)}, u32[]{:S(2)}) %all-to-all-start.2) | async-done | bytes 524320 | tf_op jit(solution)/shard_map/all_to_all | solution.py:489
  150.1 8.9 %all_to_all.25 = bf16[4,80,512]{2,1,0:T(8,128)(2,1)S(1)} all-to-all(bf16[4,80,512]{2,1,0:T(8,128)(2,1)S(1)} %bitcast.70), channel_id=1, replica_groups=mesh['seq'=8,'exp'=4] {'exp'}, dimensions={0} | all-to-all | bytes 655360 | tf_op jit(solution)/shard_map/all_to_all | solution.py:497
  159.0 2.9 %collective-permute-start.11 = (bf16[320,512]{1,0:T(8,128)(2,1)S(1)}, bf16[320,512]{1,0:T(8,128)(2,1)S(1)}, u32[]{:S(2)}, u32[]{:S(2)}) collective-permute-start(bf16[320,512]{1,0:T(8,128)(2,1)S(1)} %bitcast.63), channel_id=1, source_target_pairs={{8,0},{12,4},{16,8},{20,12},{24,16},{28,20},{0,24},{4,28},{9,1},{1... | collective-permute-start | bytes 983048 | tf_op jit(solution)/shard_map/ppermute | solution.py:392
  164.1 4.1 %collective-permute-done.11.refs_2_ = bf16[320,512]{1,0:T(8,128)(2,1)S(1)} collective-permute-done((bf16[320,512]{1,0:T(8,128)(2,1)S(1)}, bf16[320,512]{1,0:T(8,128)(2,1)S(1)}, u32[]{:S(2)}, u32[]{:S(2)}) %collective-permute-start.11) | collective-permute-done | bytes 327712 | tf_op jit(solution)/shard_map/ppermute | solution.py:392
  169.6 19.7 %collective-permute-done.13.refs_4_ = bf16[320,512]{1,0:T(8,128)(2,1)S(1)} collective-permute-done((bf16[320,512]{1,0:T(8,128)(2,1)S(1)}, bf16[320,512]{1,0:T(8,128)(2,1)S(1)}, u32[]{:S(2)}, u32[]{:S(2)}) %collective-permute-start.13) | collective-permute-done | bytes 327712 | tf_op jit(solution)/shard_map/ppermute | solution.py:392
  191.1 6.0 %collective-permute-done.14.refs_5_ = bf16[320,512]{1,0:T(8,128)(2,1)S(1)} collective-permute-done((bf16[320,512]{1,0:T(8,128)(2,1)S(1)}, bf16[320,512]{1,0:T(8,128)(2,1)S(1)}, u32[]{:S(2)}, u32[]{:S(2)}) %collective-permute-start.14) | collective-permute-done | bytes 327712 | tf_op jit(solution)/shard_map/ppermute | solution.py:400
  197.1 7.0 %collective-permute-done.16.refs_7_ = bf16[320,512]{1,0:T(8,128)(2,1)S(1)} collective-permute-done((bf16[320,512]{1,0:T(8,128)(2,1)S(1)}, bf16[320,512]{1,0:T(8,128)(2,1)S(1)}, u32[]{:S(2)}, u32[]{:S(2)}) %collective-permute-start.16) | collective-permute-done | bytes 327712 | tf_op jit(solution)/shard_map/ppermute | solution.py:400
  204.1 17.4 %expert_hidden.1 = (bf16[320,1536]{1,0:T(8,128)(2,1)S(1)}, f32[40,4096]{1,0:T(8,128)S(1)}) custom-call(s32[8]{0:T(128)S(1)} %stack.46.order_ref, s32[1]{0:T(128)} %bitcast.12.place_ref, bf16[320,512]{1,0:T(8,128)(2,1)S(1)} %bitcast.67, bf16[320,512]{1,0:T(8,128)(2,1)S(1)} %collective-permute-done.10.refs_1_, ...), custom_call_target="tpu_custom_call" | custom-call | tf_op jit(solution)/shard_map/expert_hidden/pallas_call | solution.py:283
  221.6 7.0 %expert_down.1 = (bf16[40,4096]{1,0:T(8,128)(2,1)S(1)}, bf16[40,4096]{1,0:T(8,128)(2,1)S(1)}, bf16[40,4096]{1,0:T(8,128)(2,1)S(1)}, bf16[40,4096]{1,0:T(8,128)(2...) custom-call(s32[1]{0:T(128)} %bitcast.2.z_ref, ...), custom_call_target="tpu_custom_call" | custom-call | tf_op jit(solution)/shard_map/expert_down/pallas_call | solution.py:331
  232.2 3.4 %collective-permute-done.18 = bf16[40,4096]{1,0:T(8,128)(2,1)} collective-permute-done((bf16[40,4096]{1,0:T(8,128)(2,1)S(1)}, bf16[40,4096]{1,0:T(8,128)(2,1)}, u32[]{:S(2)}, u32[]{:S(2)}) %collective-permute-start.18) | collective-permute-done | bytes 327712 | tf_op jit(solution)/shard_map/ppermute | solution.py:400
  236.6 5.8 %collective-permute-done.20 = bf16[40,4096]{1,0:T(8,128)(2,1)S(1)} collective-permute-done((bf16[40,4096]{1,0:T(8,128)(2,1)S(1)}, bf16[40,4096]{1,0:T(8,128)(2,1)S(1)}, u32[]{:S(2)}, u32[]{:S(2)}) %collective-permute-start.20) | collective-permute-done | bytes 327712 | tf_op jit(solution)/shard_map/ppermute | solution.py:400
  242.6 6.9 %collective-permute-done.22 = bf16[40,4096]{1,0:T(8,128)(2,1)S(1)} collective-permute-done((bf16[40,4096]{1,0:T(8,128)(2,1)S(1)}, bf16[40,4096]{1,0:T(8,128)(2,1)S(1)}, u32[]{:S(2)}, u32[]{:S(2)}) %collective-permute-start.22) | collective-permute-done | bytes 327712 | tf_op jit(solution)/shard_map/ppermute | solution.py:400
  249.9 6.6 %collective-permute-done.17 = bf16[40,4096]{1,0:T(8,128)(2,1)S(1)} collective-permute-done((bf16[40,4096]{1,0:T(8,128)(2,1)S(1)}, bf16[40,4096]{1,0:T(8,128)(2,1)S(1)}, u32[]{:S(2)}, u32[]{:S(2)}) %collective-permute-start.17) | collective-permute-done | bytes 327712 | tf_op jit(solution)/shard_map/ppermute | solution.py:400
  256.5 4.9 %collective-permute-done.21 = bf16[40,4096]{1,0:T(8,128)(2,1)S(1)} collective-permute-done((bf16[40,4096]{1,0:T(8,128)(2,1)S(1)}, bf16[40,4096]{1,0:T(8,128)(2,1)S(1)}, u32[]{:S(2)}, u32[]{:S(2)}) %collective-permute-start.21) | collective-permute-done | bytes 327712 | tf_op jit(solution)/shard_map/ppermute | solution.py:392
  262.5 10.0 %all-to-all-start.4 = ((bf16[4,40,1024]{2,1,0:T(8,128)(2,1)}), bf16[4,40,1024]{2,1,0:T(8,128)(2,1)S(1)}, u32[]{:S(2)}, u32[]{:S(2)}) async-start(bf16[4,40,1024]{2,1,0:T(8,128)(2,1)} %bitcast.58), calls=%async_computation.4 | async-start | bytes 655360 | tf_op jit(solution)/shard_map/all_to_all | solution.py:517
  272.6 4.7 %all-to-all-done.4 = bf16[4,40,1024]{2,1,0:T(8,128)(2,1)S(1)} async-done(((bf16[4,40,1024]{2,1,0:T(8,128)(2,1)}), bf16[4,40,1024]{2,1,0:T(8,128)(2,1)S(1)}, u32[]{:S(2)}, u32[]{:S(2)}) %all-to-all-start.4) | async-done | bytes 327712 | tf_op jit(solution)/shard_map/all_to_all | solution.py:517
  (108 shorter events, 30.8 us)
Async XLA Ops:
  0.8 7.4 %collective-permute-start.2 = (bf16[8,2048]{1,0:T(8,128)(2,1)S(1)}, bf16[8,2048]{1,0:T(8,128)(2,1)S(1)}, u32[]{:S(2)}, u32[]{:S(2)}) collective-permute-start(bf16[8,2048]{1,0:T(8,128)(2,1)S(1)} %slice.16), channel_id=1, source_target_pairs={{0,4},{4,8},{8,12},{12,16},{16,20},{20,24},{24,28},{1,5},{5,9},{9,... | collective-permute-start | bytes 98312 | tf_op jit(solution)/shard_map/ppermute | solution.py:416
  14.9 12.9 %all-to-all-start = ((f32[4,64,544]{2,1,0:T(8,128)}), f32[4,64,544]{2,1,0:T(8,128)S(1)}, u32[]{:S(2)}, u32[]{:S(2)}) async-start(f32[4,64,544]{2,1,0:T(8,128)} %broadcast_in_dim.35), calls=%async_computation | async-start | bytes 1310720 | tf_op jit(solution)/shard_map/all_to_all | solution.py:470
  36.8 29.6 %all-to-all-start.1 = ((bf16[8,32,2048]{2,1,0:T(8,128)(2,1)}), bf16[8,32,2048]{2,1,0:T(8,128)(2,1)S(1)}, u32[]{:S(2)}, u32[]{:S(2)}) async-start(bf16[8,32,2048]{2,1,0:T(8,128)(2,1)} %broadcast_in_dim.38), calls=%async_computation.1 | async-start | bytes 2097152 | tf_op jit(solution)/shard_map/all_to_all | solution.py:482
  41.4 35.1 %copy-start.5 = (bf16[64,1024]{1,0:T(8,128)(2,1)S(1)}, bf16[64,1024]{1,0:T(8,128)(2,1)}, u32[]{:S(2)}) copy-start(bf16[64,1024]{1,0:T(8,128)(2,1)} %param.27) | copy-start | bytes 393220
  41.4 42.6 %copy-start.7 = (s32[64,2]{0,1:T(2,128)S(1)}, s32[64,2]{0,1:T(2,128)}, u32[]{:S(2)}) copy-start(s32[64,2]{0,1:T(2,128)} %param.29) | copy-start | bytes 1540
  67.6 59.1 %copy-start = (bf16[2048,512]{1,0:T(8,128)(2,1)S(1)}, bf16[2048,512]{1,0:T(8,128)(2,1)}, u32[]{:S(2)}) copy-start(bf16[2048,512]{1,0:T(8,128)(2,1)} %refs_8_.1) | copy-start | bytes 6291460
  73.6 32.5 %collective-permute-start.4 = (bf16[64,2048]{1,0:T(8,128)(2,1)}, bf16[64,2048]{1,0:T(8,128)(2,1)S(1)}, u32[]{:S(2)}, u32[]{:S(2)}) collective-permute-start(bf16[64,2048]{1,0:T(8,128)(2,1)} %scan_mix.1.refs_0_), channel_id=1, source_target_pairs={{8,0},{12,4},{16,8},{20,12},{24,16},{28,20},{0,24},{4,28},{9,1},{1... | collective-permute-start | bytes 786440 | tf_op jit(solution)/shard_map/ppermute | solution.py:392
  76.2 31.3 %collective-permute-start.6 = (bf16[64,2048]{1,0:T(8,128)(2,1)}, bf16[64,2048]{1,0:T(8,128)(2,1)S(1)}, u32[]{:S(2)}, u32[]{:S(2)}) collective-permute-start(bf16[64,2048]{1,0:T(8,128)(2,1)} %scan_mix.1.refs_0_), channel_id=1, source_target_pairs={{16,0},{20,4},{24,8},{28,12},{0,16},{4,20},{8,24},{12,28},{17,1},{... | collective-permute-start | bytes 786440 | tf_op jit(solution)/shard_map/ppermute | solution.py:392
  76.2 31.4 %collective-permute-start.8 = (bf16[64,2048]{1,0:T(8,128)(2,1)}, bf16[64,2048]{1,0:T(8,128)(2,1)S(1)}, u32[]{:S(2)}, u32[]{:S(2)}) collective-permute-start(bf16[64,2048]{1,0:T(8,128)(2,1)} %scan_mix.1.refs_0_), channel_id=1, source_target_pairs={{24,0},{28,4},{0,8},{4,12},{8,16},{12,20},{16,24},{20,28},{25,1},{... | collective-permute-start | bytes 786440 | tf_op jit(solution)/shard_map/ppermute | solution.py:392
  77.6 65.3 %collective-permute-start = (bf16[64,512]{1,0:T(8,128)(2,1)}, bf16[64,512]{1,0:T(8,128)(2,1)}, u32[]{:S(2)}, u32[]{:S(2)}) collective-permute-start(bf16[64,512]{1,0:T(8,128)(2,1)} %bitcast.60), channel_id=1, source_target_pairs={{0,0},{8,1},{16,2},{24,3},{4,4},{12,5},{20,6},{28,7},{1,8},{9,9},{... | collective-permute-start | bytes 196616 | tf_op jit(solution)/shard_map/ppermute | solution.py:430
  106.1 5.5 %collective-permute-start.3 = (bf16[64,2048]{1,0:T(8,128)(2,1)}, bf16[64,2048]{1,0:T(8,128)(2,1)S(1)}, u32[]{:S(2)}, u32[]{:S(2)}) collective-permute-start(bf16[64,2048]{1,0:T(8,128)(2,1)} %scan_mix.1.refs_0_), channel_id=1, source_target_pairs={{4,0},{0,4},{12,8},{8,12},{20,16},{16,20},{28,24},{24,28},{5,1},{1... | collective-permute-start | bytes 786440 | tf_op jit(solution)/shard_map/ppermute | solution.py:400
  106.1 16.4 %collective-permute-start.5 = (bf16[64,2048]{1,0:T(8,128)(2,1)S(1)}, bf16[64,2048]{1,0:T(8,128)(2,1)S(1)}, u32[]{:S(2)}, u32[]{:S(2)}) collective-permute-start(bf16[64,2048]{1,0:T(8,128)(2,1)S(1)} %collective-permute-done.4.refs_2_), channel_id=1, source_target_pairs={{4,0},{0,4},{12,8},{8,12},{20,16},{16,20},{28,24},{24,28},{5,1},{1... | collective-permute-start | bytes 786440 | tf_op jit(solution)/shard_map/ppermute | solution.py:400
  107.5 15.0 %collective-permute-start.7 = (bf16[64,2048]{1,0:T(8,128)(2,1)S(1)}, bf16[64,2048]{1,0:T(8,128)(2,1)}, u32[]{:S(2)}, u32[]{:S(2)}) collective-permute-start(bf16[64,2048]{1,0:T(8,128)(2,1)S(1)} %collective-permute-done.6.refs_4_), channel_id=1, source_target_pairs={{4,0},{0,4},{12,8},{8,12},{20,16},{16,20},{28,24},{24,28},{5,1},{1... | collective-permute-start | bytes 786440 | tf_op jit(solution)/shard_map/ppermute | solution.py:400
  107.6 19.1 %collective-permute-start.9 = (bf16[64,2048]{1,0:T(8,128)(2,1)S(1)}, bf16[64,2048]{1,0:T(8,128)(2,1)}, u32[]{:S(2)}, u32[]{:S(2)}) collective-permute-start(bf16[64,2048]{1,0:T(8,128)(2,1)S(1)} %collective-permute-done.8.refs_6_), channel_id=1, source_target_pairs={{4,0},{0,4},{12,8},{8,12},{20,16},{16,20},{28,24},{24,28},{5,1},{1... | collective-permute-start | bytes 786440 | tf_op jit(solution)/shard_map/ppermute | solution.py:400
  111.5 31.4 %collective-permute-start.1 = (bf16[64,512]{1,0:T(8,128)(2,1)}, bf16[64,512]{1,0:T(8,128)(2,1)S(1)}, u32[]{:S(2)}, u32[]{:S(2)}) collective-permute-start(bf16[64,512]{1,0:T(8,128)(2,1)} %bitcast.73), channel_id=1, source_target_pairs={{4,0},{12,1},{20,2},{28,3},{0,4},{8,5},{16,6},{24,7},{5,8},{13,9},... | collective-permute-start | bytes 196616 | tf_op jit(solution)/shard_map/ppermute | solution.py:430
  130.9 73.2 %copy-start.2 = (f32[4096]{0:T(1024)S(1)}, f32[4096]{0:T(1024)}, u32[]{:S(2)}) copy-start(f32[4096]{0:T(1024)} %param.28) | copy-start | bytes 49156
  130.9 18.9 %all-to-all-start.2 = ((bf16[4,128,512]{2,1,0:T(8,128)(2,1)}), bf16[4,128,512]{2,1,0:T(8,128)(2,1)S(1)}, u32[]{:S(2)}, u32[]{:S(2)}) async-start(bf16[4,128,512]{2,1,0:T(8,128)(2,1)} %bitcast.23), calls=%async_computation.2 | async-start | bytes 1048576 | tf_op jit(solution)/shard_map/all_to_all | solution.py:489
  159.0 9.2 %collective-permute-start.11 = (bf16[320,512]{1,0:T(8,128)(2,1)S(1)}, bf16[320,512]{1,0:T(8,128)(2,1)S(1)}, u32[]{:S(2)}, u32[]{:S(2)}) collective-permute-start(bf16[320,512]{1,0:T(8,128)(2,1)S(1)} %bitcast.63), channel_id=1, source_target_pairs={{8,0},{12,4},{16,8},{20,12},{24,16},{28,20},{0,24},{4,28},{9,1},{1... | collective-permute-start | bytes 983048 | tf_op jit(solution)/shard_map/ppermute | solution.py:392
  161.9 27.5 %collective-permute-start.13 = (bf16[320,512]{1,0:T(8,128)(2,1)S(1)}, bf16[320,512]{1,0:T(8,128)(2,1)S(1)}, u32[]{:S(2)}, u32[]{:S(2)}) collective-permute-start(bf16[320,512]{1,0:T(8,128)(2,1)S(1)} %bitcast.64), channel_id=1, source_target_pairs={{16,0},{20,4},{24,8},{28,12},{0,16},{4,20},{8,24},{12,28},{17,1},{... | collective-permute-start | bytes 983048 | tf_op jit(solution)/shard_map/ppermute | solution.py:392
  161.9 29.0 %collective-permute-start.15 = (bf16[320,512]{1,0:T(8,128)(2,1)S(1)}, bf16[320,512]{1,0:T(8,128)(2,1)S(1)}, u32[]{:S(2)}, u32[]{:S(2)}) collective-permute-start(bf16[320,512]{1,0:T(8,128)(2,1)S(1)} %bitcast.65), channel_id=1, source_target_pairs={{24,0},{28,4},{0,8},{4,12},{8,16},{12,20},{16,24},{20,28},{25,1},{... | collective-permute-start | bytes 983048 | tf_op jit(solution)/shard_map/ppermute | solution.py:392
  162.6 28.5 %collective-permute-start.10 = (bf16[320,512]{1,0:T(8,128)(2,1)S(1)}, bf16[320,512]{1,0:T(8,128)(2,1)S(1)}, u32[]{:S(2)}, u32[]{:S(2)}) collective-permute-start(bf16[320,512]{1,0:T(8,128)(2,1)S(1)} %bitcast.66), channel_id=1, source_target_pairs={{4,0},{0,4},{12,8},{8,12},{20,16},{16,20},{28,24},{24,28},{5,1},{1... | collective-permute-start | bytes 983048 | tf_op jit(solution)/shard_map/ppermute | solution.py:400
  168.2 23.0 %collective-permute-start.12 = (bf16[320,512]{1,0:T(8,128)(2,1)S(1)}, bf16[320,512]{1,0:T(8,128)(2,1)S(1)}, u32[]{:S(2)}, u32[]{:S(2)}) collective-permute-start(bf16[320,512]{1,0:T(8,128)(2,1)S(1)} %collective-permute-done.11.refs_2_), channel_id=1, source_target_pairs={{4,0},{0,4},{12,8},{8,12},{20,16},{16,20},{28,24},{24,28},{5,1},{1... | collective-permute-start | bytes 983048 | tf_op jit(solution)/shard_map/ppermute | solution.py:400
  189.4 7.7 %collective-permute-start.14 = (bf16[320,512]{1,0:T(8,128)(2,1)S(1)}, bf16[320,512]{1,0:T(8,128)(2,1)S(1)}, u32[]{:S(2)}, u32[]{:S(2)}) collective-permute-start(bf16[320,512]{1,0:T(8,128)(2,1)S(1)} %collective-permute-done.13.refs_4_), channel_id=1, source_target_pairs={{4,0},{0,4},{12,8},{8,12},{20,16},{16,20},{28,24},{24,28},{5,1},{1... | collective-permute-start | bytes 983048 | tf_op jit(solution)/shard_map/ppermute | solution.py:400
  190.9 13.3 %collective-permute-start.16 = (bf16[320,512]{1,0:T(8,128)(2,1)S(1)}, bf16[320,512]{1,0:T(8,128)(2,1)S(1)}, u32[]{:S(2)}, u32[]{:S(2)}) collective-permute-start(bf16[320,512]{1,0:T(8,128)(2,1)S(1)} %collective-permute-done.15.refs_6_), channel_id=1, source_target_pairs={{4,0},{0,4},{12,8},{8,12},{20,16},{16,20},{28,24},{24,28},{5,1},{1... | collective-permute-start | bytes 983048 | tf_op jit(solution)/shard_map/ppermute | solution.py:400
  228.6 7.0 %collective-permute-start.18 = (bf16[40,4096]{1,0:T(8,128)(2,1)S(1)}, bf16[40,4096]{1,0:T(8,128)(2,1)}, u32[]{:S(2)}, u32[]{:S(2)}) collective-permute-start(bf16[40,4096]{1,0:T(8,128)(2,1)S(1)} %get-tuple-element.27), channel_id=1, source_target_pairs={{4,0},{0,4},{12,8},{8,12},{20,16},{16,20},{28,24},{24,28},{5,1},{1... | collective-permute-start | bytes 983048 | tf_op jit(solution)/shard_map/ppermute | solution.py:400
  230.6 11.9 %collective-permute-start.20 = (bf16[40,4096]{1,0:T(8,128)(2,1)S(1)}, bf16[40,4096]{1,0:T(8,128)(2,1)S(1)}, u32[]{:S(2)}, u32[]{:S(2)}) collective-permute-start(bf16[40,4096]{1,0:T(8,128)(2,1)S(1)} %get-tuple-element.29), channel_id=1, source_target_pairs={{4,0},{0,4},{12,8},{8,12},{20,16},{16,20},{28,24},{24,28},{5,1},{1... | collective-permute-start | bytes 983048 | tf_op jit(solution)/shard_map/ppermute | solution.py:400
  230.6 18.8 %collective-permute-start.22 = (bf16[40,4096]{1,0:T(8,128)(2,1)S(1)}, bf16[40,4096]{1,0:T(8,128)(2,1)S(1)}, u32[]{:S(2)}, u32[]{:S(2)}) collective-permute-start(bf16[40,4096]{1,0:T(8,128)(2,1)S(1)} %get-tuple-element.31), channel_id=1, source_target_pairs={{4,0},{0,4},{12,8},{8,12},{20,16},{16,20},{28,24},{24,28},{5,1},{1... | collective-permute-start | bytes 983048 | tf_op jit(solution)/shard_map/ppermute | solution.py:400
  232.1 24.4 %collective-permute-start.17 = (bf16[40,4096]{1,0:T(8,128)(2,1)S(1)}, bf16[40,4096]{1,0:T(8,128)(2,1)S(1)}, u32[]{:S(2)}, u32[]{:S(2)}) collective-permute-start(bf16[40,4096]{1,0:T(8,128)(2,1)S(1)} %get-tuple-element.25), channel_id=1, source_target_pairs={{4,0},{0,4},{12,8},{8,12},{20,16},{16,20},{28,24},{24,28},{5,1},{1... | collective-permute-start | bytes 983048 | tf_op jit(solution)/shard_map/ppermute | solution.py:400
  236.6 19.9 %collective-permute-start.19 = (bf16[40,4096]{1,0:T(8,128)(2,1)S(1)}, bf16[40,4096]{1,0:T(8,128)(2,1)S(1)}, u32[]{:S(2)}, u32[]{:S(2)}) collective-permute-start(bf16[40,4096]{1,0:T(8,128)(2,1)S(1)} %add_convert_fusion.4), channel_id=1, source_target_pairs={{24,0},{28,4},{0,8},{4,12},{8,16},{12,20},{16,24},{20,28},{25,1},{... | collective-permute-start | bytes 983048 | tf_op jit(solution)/shard_map/ppermute | solution.py:392
  242.5 18.8 %collective-permute-start.21 = (bf16[40,4096]{1,0:T(8,128)(2,1)S(1)}, bf16[40,4096]{1,0:T(8,128)(2,1)S(1)}, u32[]{:S(2)}, u32[]{:S(2)}) collective-permute-start(bf16[40,4096]{1,0:T(8,128)(2,1)S(1)} %add_convert_fusion.3), channel_id=1, source_target_pairs={{16,0},{20,4},{24,8},{28,12},{0,16},{4,20},{8,24},{12,28},{17,1},{... | collective-permute-start | bytes 983048 | tf_op jit(solution)/shard_map/ppermute | solution.py:392
  249.5 11.9 %collective-permute-start.23 = (bf16[40,4096]{1,0:T(8,128)(2,1)S(1)}, bf16[40,4096]{1,0:T(8,128)(2,1)S(1)}, u32[]{:S(2)}, u32[]{:S(2)}) collective-permute-start(bf16[40,4096]{1,0:T(8,128)(2,1)S(1)} %add_convert_fusion.2), channel_id=1, source_target_pairs={{8,0},{12,4},{16,8},{20,12},{24,16},{28,20},{0,24},{4,28},{9,1},{1... | collective-permute-start | bytes 983048 | tf_op jit(solution)/shard_map/ppermute | solution.py:392
  262.5 14.8 %all-to-all-start.4 = ((bf16[4,40,1024]{2,1,0:T(8,128)(2,1)}), bf16[4,40,1024]{2,1,0:T(8,128)(2,1)S(1)}, u32[]{:S(2)}, u32[]{:S(2)}) async-start(bf16[4,40,1024]{2,1,0:T(8,128)(2,1)} %bitcast.58), calls=%async_computation.4 | async-start | bytes 655360 | tf_op jit(solution)/shard_map/all_to_all | solution.py:517
  (8 other events, 87.4 us)
